TPU v7x, 256 devices: a whole 4x4x8 slice. The times are simulated.
256 devices in a mesh: expert: 32 (over z, x), tensor: 8 (over y, core).
Axes of the slice: x: 4, y: 4, z: 8, core: 2. Of those that a mesh axis runs over, the one named last changes fastest.
Arguments:
- tokens: bfloat16 [2048, 8192], P('expert', 'tensor'), may hold values from -6 to 6
- frozen_gate_weight: bfloat16 [8192, 28672], P('tensor', 'expert'), may hold values from -0.0625 to 0.0625
- frozen_up_weight: bfloat16 [8192, 28672], P('tensor', 'expert'), may hold values from -0.0625 to 0.0625
- frozen_down_weight: bfloat16 [28672, 8192], P('expert', 'tensor'), may hold values from -0.03125 to 0.03125
- adapter_down_weight: bfloat16 [128, 8192, 128], P('expert', 'tensor'), may hold values from -0.0625 to 0.0625
- adapter_up_weight: bfloat16 [128, 128, 8192], P('expert', None, 'tensor'), may hold values from -0.0625 to 0.0625
- routes: int32 [2048, 2], P('expert'), may hold values from 0 to 127, all different within a row; in each aligned block of 64 rows (0 to 63, 64 to 127, ...) at most 2 rows name the same one
- route_gate_weights: float32 [2048, 2], P('expert'), may hold values from 0.1 to 1
- output_gradient: bfloat16 [2048, 8192], P('expert', 'tensor'), may hold values from -6 to 6
Outputs:
- ffn_out: bfloat16 [2048, 8192], P('expert', 'tensor')
- grad_down: bfloat16 [128, 8192, 128], P('expert', 'tensor')
- grad_up: bfloat16 [128, 128, 8192], P('expert', None, 'tensor')
Inputs may be any that keep to these rules, and one draw needn't show every extreme that they name: `routes`: the two experts of a token differ. Among the 64 rows of one index of expert no expert is named more than 2 times, and in some such rows one expert is named exactly 2 times.
All inputs are finite; a program needn't handle non-finite values.
Results may differ from a plain program's by a relative error of at most 0.025.
Values may be sent and summed in bfloat16 or wider, within the bound.
No kernel may reach another device: no remote copies, remote signals or barrier semaphores. Data moves between devices by JAX's collectives and lax.ppermute only.
A program may use at most 64 MiB of HBM per device.

v0:
```python
import jax
import jax.numpy as jnp
from jax import lax
from jax.sharding import Mesh, PartitionSpec as P

BF = jnp.bfloat16
F32 = jnp.float32
NZ, NX, NY, NC = 8, 4, 4, 2


def tie(value, *after):
    return lax.optimization_barrier((value,) + after)[0]


def from_peer(value, axis, offset):
    n = lax.axis_size(axis)
    return lax.ppermute(value, axis, [(i, (i - offset) % n) for i in range(n)])


def direct_gather(value, axis):
    n = lax.axis_size(axis)
    return [value] + [from_peer(value, axis, d) for d in range(1, n)]


def plus(a, b):
    return (a.astype(F32) + b.astype(F32)).astype(BF)


def ring_reduce(blocks, axis, beside):
    n = lax.axis_size(axis)
    far = {1: n // 2, -1: (n - 1) // 2}
    moving = {sign: blocks[(sign * far[sign]) % n] for sign in far}
    for d in range(n // 2 - 1, -1, -1):
        if d == 1:
            moving[1], moving[-1], beside = lax.optimization_barrier((moving[1], moving[-1], beside))
        for sign in far:
            if d < far[sign]:
                moving[sign] = from_peer(moving[sign], axis, -sign)
                if d:
                    moving[sign] = plus(moving[sign], blocks[(sign * d) % n])
    return blocks[0].astype(F32) + moving[1].astype(F32) + moving[-1].astype(F32), beside


def ring_gather(values, axis):
    n = lax.axis_size(axis)
    held = [[value] + [None] * (n - 1) for value in values]
    up, down = list(values), list(values)
    for step in range(1, n // 2 + 1):
        for i in range(len(values)):
            if step > 2:
                behind = held[1 - i][step - 2 + i]
                up[i], down[i], behind = lax.optimization_barrier((up[i], down[i], behind))
                held[1 - i][step - 2 + i] = behind
            up[i] = from_peer(up[i], axis, 1)
            held[i][step] = up[i]
            if step <= (n - 1) // 2:
                down[i] = from_peer(down[i], axis, -1)
                held[i][n - step] = down[i]
    return jnp.concatenate([block for blocks in held for block in blocks], 0)


def gather_tokens(tokens):
    blocks = direct_gather(tokens, "x")
    return ring_gather([jnp.concatenate(blocks[:2], 0), jnp.concatenate(blocks[2:], 0)], "z")


def row_of(z, x, place, rows):
    dz, dx = (z - lax.axis_index("z")) % NZ, (x - lax.axis_index("x")) % NX
    return ((dx // 2 * NZ + dz) * 2 + dx % 2) * rows + place


def in_order(out):
    return jnp.concatenate([block_rows(out, half * NZ + dz) for dz in range(NZ) for half in (0, 1)], 0)


def block_rows(out, index):
    step = out.shape[0] // (2 * NY * NC)
    device = index // 2
    place = (device // NC - lax.axis_index("y")) % NY * NC + (device % NC - lax.axis_index("c")) % NC
    return lax.dynamic_slice_in_dim(out, (place * 2 + index % 2) * step, step, 0)


def exchange(blocks, axis):
    return lax.all_to_all(blocks, axis, split_axis=0, concat_axis=0, tiled=True)


def reduce_rows(out):
    rows, width = out.shape
    cut, step = width * 5 // 8, rows // NZ
    near = out[:, cut:].reshape(NZ, NX, step // NX, width - cut)
    near = jnp.concatenate([near[:, d].reshape(-1, width - cut) for d in range(NX)], 0)
    near = direct_reduce(near, "x").astype(BF)
    far, near = ring_reduce([out[d * step : (d + 1) * step, :cut] for d in range(NZ)], "z", near)
    far = far.astype(BF)
    step = near.shape[0] // NZ
    turn = (NZ - lax.axis_index("z")) % NZ * step
    near = lax.dynamic_slice_in_dim(jnp.concatenate([near, near], 0), turn, NZ * step, 0)
    near = jnp.sum(exchange(near.reshape(NZ, step, width - cut), "z").astype(F32), 0)
    return jnp.concatenate([direct_reduce(far, "x"), near], 1)


def direct_reduce(part, axis):
    n = lax.axis_size(axis)
    step = part.shape[0] // n
    total = part[:step].astype(F32)
    for d in range(1, n):
        total = total + from_peer(part[d * step : (d + 1) * step], axis, -d).astype(F32)
    return total


def gather_hidden(hidden):
    return [jnp.concatenate([piece, from_peer(piece, "c", 1)], 0) for piece in direct_gather(hidden, "y")]


def sum_over_tensor(part):
    pair = plus(part, from_peer(part, "c", 1))
    total = pair.astype(F32)
    for d in (1, 3, 2):
        total = total + from_peer(pair, "y", d).astype(F32)
    return total.astype(BF)


def per_device(
    tokens,
    frozen_gate_weight,
    frozen_up_weight,
    frozen_down_weight,
    adapter_down_weight,
    adapter_up_weight,
    routes,
    route_gate_weights,
    output_gradient,
):
    tok_count, width = tokens.shape
    hidden_width = frozen_gate_weight.shape[1]
    resident = adapter_down_weight.shape[0]
    peers = NZ * NX
    most = 2
    per_peer = resident * most
    slots = peers * per_peer
    all_rows = peers * tok_count

    with jax.named_scope("gather_tokens"):
        shard_rows = gather_tokens(tokens)
    gate_up_weight = jnp.concatenate([frozen_gate_weight, frozen_up_weight], 1)

    with jax.named_scope("gate_up"):
        partial_value = jnp.dot(shard_rows, gate_up_weight, preferred_element_type=F32).astype(BF)
    with jax.named_scope("reduce_gate_up"):
        summed = lax.psum_scatter(
            partial_value, ("y", "c"), scatter_dimension=0, tiled=True
        ).astype(F32)
    with jax.named_scope("activate"):
        hidden = (jax.nn.silu(summed[:, :hidden_width]) * summed[:, hidden_width:]).astype(BF)

    with jax.named_scope("routing"):
        ids = routes.reshape(-1)
        pairs = ids.shape[0]
        pair = jnp.arange(pairs, dtype=jnp.int32)
        same = (ids[:, None] == ids[None, :]) & (pair[:, None] > pair[None, :])
        target = ids * most + jnp.sum(same.astype(jnp.int32), axis=1)
        slot = jnp.arange(slots, dtype=jnp.int32)
        select = (slot[:, None] == target[None, :]).astype(BF)
        scaled = (route_gate_weights[:, :, None] * output_gradient[:, None, :].astype(F32)).astype(BF)
        scaled = scaled.reshape(pairs, width)
        weight = route_gate_weights.reshape(pairs, 1)
        high = weight.astype(BF)
        rest = weight - high.astype(F32)
        middle = rest.astype(BF)
        low_bits = (rest - middle.astype(F32)).astype(BF)
        place = (pair // 2 + 1).astype(BF).reshape(pairs, 1)
        extra = jnp.concatenate(
            [place, high, middle, low_bits, jnp.zeros((pairs, 124), BF)], 1
        )
        send = jnp.dot(select, jnp.concatenate([scaled, extra], 1), preferred_element_type=F32)
        send = send.astype(BF).reshape(peers, per_peer, width + 128)
    with jax.named_scope("exchange_gradients"):
        send = tie(send, partial_value)
        got = lax.all_to_all(send, ("z", "x"), split_axis=0, concat_axis=0, tiled=True)
    with jax.named_scope("slots"):
        got = got.reshape(peers, resident, most, width + 128).transpose(1, 0, 2, 3)
        got = got.reshape(resident, peers * most, width + 128)
        incoming_gradients = got[:, :, :width]
        extra = got[:, :, width : width + 4].astype(F32).reshape(resident * peers * most, 4)
        place = extra[:, 0].astype(jnp.int32) - 1
        weight = extra[:, 1] + extra[:, 2] + extra[:, 3]
        source = (jnp.arange(resident * peers * most, dtype=jnp.int32) // most) % peers
        z, x = source // NX, source % NX
        row = row_of(z, x, place, tok_count)
        row = jnp.where(place < 0, -1, row)
        rows = jnp.arange(all_rows, dtype=jnp.int32)
        pick = (row[:, None] == rows[None, :]).astype(BF)
        block = all_rows // (NY * NC)
        device = rows // block
        device = (device // NC + lax.axis_index("y")) % NY * NC + (device + lax.axis_index("c")) % NC
        held_row = device * block + rows % block
        put = (held_row[:, None] == row[None, :]).astype(BF)

    with jax.named_scope("low_rank"):
        incoming_rows = jnp.dot(pick, shard_rows, preferred_element_type=F32)
        incoming_rows = incoming_rows.astype(BF)
        incoming_rows = incoming_rows.reshape(resident, peers * most, width)
        low = jnp.einsum(
            "csk,cko->cso", incoming_rows, adapter_down_weight, preferred_element_type=F32
        ).astype(BF)
        back = jnp.einsum(
            "csf,cxf->csx", incoming_gradients, adapter_up_weight, preferred_element_type=F32
        ).astype(BF)
    with jax.named_scope("sum_low_rank"):
        both = sum_over_tensor(jnp.concatenate([low, back], 0))
        low, back = both[:resident], both[resident:]
    with jax.named_scope("adapter_out"):
        expert_out = jnp.einsum(
            "csx,cxo->cso", low, adapter_up_weight, preferred_element_type=F32
        ).astype(BF)
        expert_out = expert_out.reshape(slots, width)
        weighted = (weight[:, None] * expert_out.astype(F32)).astype(BF)
    with jax.named_scope("adapter_grads"):
        grad_up = jnp.einsum(
            "csr,csd->crd", low, incoming_gradients, preferred_element_type=F32
        ).astype(BF)
        grad_down = jnp.einsum(
            "csd,csr->cdr", incoming_rows, back, preferred_element_type=F32
        ).astype(BF)

    with jax.named_scope("gather_hidden"):
        pieces = gather_hidden(hidden)
    with jax.named_scope("down"):
        down_weight = jnp.concatenate([frozen_down_weight, weighted], 0)
        put = put.reshape(NY, -1, slots)
        out = [
            jnp.dot(
                jnp.concatenate([piece, put[d]], 1), down_weight, preferred_element_type=F32
            ).astype(BF)
            for d, piece in enumerate(pieces)
        ]
        out = jnp.concatenate(out, 0)
        out, grad_up, grad_down = lax.optimization_barrier((out, grad_up, grad_down))
    with jax.named_scope("reduce_rows"):
        ffn_out = reduce_rows(in_order(out)).astype(BF)
    return (ffn_out, grad_down, grad_up)


def solution(mesh):
    split = Mesh(mesh.devices.reshape(NZ, NX, NY, NC), ("z", "x", "y", "c"))
    e, t = ("z", "x"), ("y", "c")
    placed = (
        P(e, t),
        P(t, e),
        P(t, e),
        P(e, t),
        P(e, t, None),
        P(e, None, t),
        P(e, None),
        P(e, None),
        P(e, t),
    )
    return jax.shard_map(
        per_device,
        mesh=split,
        in_specs=placed,
        out_specs=(P(e, t), P(e, t, None), P(e, None, t)),
        check_vma=False,
    )
```

profile of v0, /device:TPU:8, one launch (start us, length us, event | category | flops | bytes accessed | tf_op | source)
XLA Modules:
  0.0 245.8 jit_solution(16625306995466033360)
XLA Ops:
  16.0 5.9 %collective-permute-start.1 = (bf16[128,1024]{1,0:T(8,128)(2,1)S(1)}, bf16[128,1024]{1,0:T(8,128)(2,1)S(1)}, u32[]{:S(2)}, u32[]{:S(2)}) collective-permute-start(bf16[128,1024]{1,0:T(8,128)(2,1)S(1)} %get-tuple-element.84), channel_id=1, source_target_pairs={{0,224},{32,0},{64,32},{96,64},{128,96},{160,128},{192,160},{224,1... | collective-permute-start | bytes 786440 | tf_op jit(solution)/shard_map/gather_tokens/ppermute | solution.py:17
  22.0 3.5 %collective-permute-start.4 = (bf16[128,1024]{1,0:T(8,128)(2,1)S(1)}, bf16[128,1024]{1,0:T(8,128)(2,1)S(1)}, u32[]{:S(2)}, u32[]{:S(2)}) collective-permute-start(bf16[128,1024]{1,0:T(8,128)(2,1)S(1)} %constant_dynamic-update-slice_fusion.2), channel_id=1, source_target_pairs={{0,224},{32,0},{64,32},{96,64},{128,96},{160,128},{192,160},{224,1... | collective-permute-start | bytes 786440 | tf_op jit(solution)/shard_map/gather_tokens/ppermute | solution.py:17
  26.2 3.7 %collective-permute-start.8 = (bf16[128,1024]{1,0:T(8,128)(2,1)S(1)}, bf16[128,1024]{1,0:T(8,128)(2,1)S(1)}, u32[]{:S(2)}, u32[]{:S(2)}) collective-permute-start(bf16[128,1024]{1,0:T(8,128)(2,1)S(1)} %collective-permute-done.1), channel_id=1, source_target_pairs={{0,224},{32,0},{64,32},{96,64},{128,96},{160,128},{192,160},{224,1... | collective-permute-start | bytes 786440 | tf_op jit(solution)/shard_map/gather_tokens/ppermute | solution.py:17
  32.2 3.7 %collective-permute-start.5 = (bf16[128,1024]{1,0:T(8,128)(2,1)S(1)}, bf16[128,1024]{1,0:T(8,128)(2,1)S(1)}, u32[]{:S(2)}, u32[]{:S(2)}) collective-permute-start(bf16[128,1024]{1,0:T(8,128)(2,1)S(1)} %collective-permute-done.4), channel_id=1, source_target_pairs={{0,224},{32,0},{64,32},{96,64},{128,96},{160,128},{192,160},{224,1... | collective-permute-start | bytes 786440 | tf_op jit(solution)/shard_map/gather_tokens/ppermute | solution.py:17
  37.8 3.7 %collective-permute-done.12 = bf16[128,1024]{1,0:T(8,128)(2,1)S(1)} collective-permute-done((bf16[128,1024]{1,0:T(8,128)(2,1)S(1)}, bf16[128,1024]{1,0:T(8,128)(2,1)S(1)}, u32[]{:S(2)}, u32[]{:S(2)}) %collective-permute-start.12) | collective-permute-done | bytes 262176 | tf_op jit(solution)/shard_map/gather_tokens/ppermute | solution.py:17
  43.6 3.6 %collective-permute-done.7 = bf16[128,1024]{1,0:T(8,128)(2,1)S(1)} collective-permute-done((bf16[128,1024]{1,0:T(8,128)(2,1)S(1)}, bf16[128,1024]{1,0:T(8,128)(2,1)S(1)}, u32[]{:S(2)}, u32[]{:S(2)}) %collective-permute-start.7) | collective-permute-done | bytes 262176 | tf_op jit(solution)/shard_map/gather_tokens/ppermute | solution.py:17
  49.2 3.6 %collective-permute-done.14 = bf16[128,1024]{1,0:T(8,128)(2,1)S(1)} collective-permute-done((bf16[128,1024]{1,0:T(8,128)(2,1)S(1)}, bf16[128,1024]{1,0:T(8,128)(2,1)S(1)}, u32[]{:S(2)}, u32[]{:S(2)}) %collective-permute-start.14) | collective-permute-done | bytes 262176 | tf_op jit(solution)/shard_map/gather_tokens/ppermute | solution.py:17
  60.5 4.9 %collective-permute-done.16 = bf16[128,1024]{1,0:T(8,128)(2,1)S(1)} collective-permute-done((bf16[128,1024]{1,0:T(8,128)(2,1)S(1)}, bf16[128,1024]{1,0:T(8,128)(2,1)S(1)}, u32[]{:S(2)}, u32[]{:S(2)}) %collective-permute-start.16) | collective-permute-done | bytes 262176 | tf_op jit(solution)/shard_map/gather_tokens/ppermute | solution.py:17
  67.5 9.6 %convolution_convert_fusion = bf16[2048,1792]{1,0:T(8,128)(2,1)} fusion(bf16[2048,1024]{1,0:T(8,128)(2,1)S(1)} %constant_dynamic-update-slice_fusion.4, bf16[1024,896]{1,0:T(8,128)(2,1)S(1)} %copy-done.9, bf16[1024,896]{1,0:T(8,128)(2,1)S(1)} %copy-done.10), kind=kOutput, calls=%fused_computation | convolution fusion | flops 7527202816 | bytes 15204352 | tf_op jit(solution)/shard_map/gate_up/dot_general | solution.py:148
  80.9 9.2 %all-to-all-start = ((bf16[32,8,1152]{2,1,0:T(8,128)(2,1)}), bf16[32,8,1152]{2,1,0:T(8,128)(2,1)S(1)}, u32[]{:S(2)}, u32[]{:S(2)}) async-start(bf16[32,8,1152]{2,1,0:T(8,128)(2,1)} %fusion.3), calls=%async_computation.1 | async-start | bytes 1179648 | tf_op jit(solution)/shard_map/exchange_gradients/all_to_all | solution.py:179
  90.3 17.4 %all-to-all-done = bf16[32,8,1152]{2,1,0:T(8,128)(2,1)S(1)} async-done(((bf16[32,8,1152]{2,1,0:T(8,128)(2,1)}), bf16[32,8,1152]{2,1,0:T(8,128)(2,1)S(1)}, u32[]{:S(2)}, u32[]{:S(2)}) %all-to-all-start) | async-done | bytes 589856 | tf_op jit(solution)/shard_map/exchange_gradients/all_to_all | solution.py:179
  109.5 3.6 %fusion.5 = bf16[256,1024]{1,0:T(8,128)(2,1)S(1)} fusion(bf16[2048,1024]{1,0:T(8,128)(2,1)} %copy-done.6, s32[256]{0:T(256)S(1)} %bitcast.42), kind=kOutput, calls=%fused_computation.17 | convolution fusion | flops 1074528256 | bytes 4719616 | tf_op jit(solution)/shard_map/low_rank/dot_general | solution.py:200
  119.5 5.0 %collective-permute-done.21 = bf16[8,64,128]{2,1,0:T(8,128)(2,1)S(1)} collective-permute-done((bf16[8,64,128]{2,1,0:T(8,128)(2,1)S(1)}, bf16[8,64,128]{2,1,0:T(8,128)(2,1)S(1)}, u32[]{:S(2)}, u32[]{:S(2)}) %collective-permute-start.21) | collective-permute-done | bytes 131104 | tf_op jit(solution)/shard_map/sum_low_rank/ppermute | solution.py:17
  124.5 4.1 %collective-permute-done.20 = bf16[8,64,128]{2,1,0:T(8,128)(2,1)S(1)} collective-permute-done((bf16[8,64,128]{2,1,0:T(8,128)(2,1)S(1)}, bf16[8,64,128]{2,1,0:T(8,128)(2,1)S(1)}, u32[]{:S(2)}, u32[]{:S(2)}) %collective-permute-start.20) | collective-permute-done | bytes 131104 | tf_op jit(solution)/shard_map/sum_low_rank/ppermute | solution.py:17
  133.0 10.6 %collective-permute-start.26 = (bf16[256,896]{1,0:T(8,128)(2,1)S(1)}, bf16[256,896]{1,0:T(8,128)(2,1)S(1)}, u32[]{:S(2)}, u32[]{:S(2)}) collective-permute-start(bf16[256,896]{1,0:T(8,128)(2,1)S(1)} %fusion.28), channel_id=1, source_target_pairs={{0,2},{2,4},{4,6},{6,0},{1,3},{3,5},{5,7},{7,1},{8,10},{10,12},{12... | collective-permute-start | bytes 1376264 | tf_op jit(solution)/shard_map/gather_hidden/ppermute | solution.py:17
  145.0 3.3 %collective-permute-start.24 = (bf16[256,896]{1,0:T(8,128)(2,1)S(1)}, bf16[256,896]{1,0:T(8,128)(2,1)S(1)}, u32[]{:S(2)}, u32[]{:S(2)}) collective-permute-start(bf16[256,896]{1,0:T(8,128)(2,1)S(1)} %fusion.28), channel_id=1, source_target_pairs={{0,4},{2,6},{4,0},{6,2},{1,5},{3,7},{5,1},{7,3},{8,12},{10,14},{12... | collective-permute-start | bytes 1376264 | tf_op jit(solution)/shard_map/gather_hidden/ppermute | solution.py:17
  150.0 6.0 %collective-permute-done.26 = bf16[256,896]{1,0:T(8,128)(2,1)S(1)} collective-permute-done((bf16[256,896]{1,0:T(8,128)(2,1)S(1)}, bf16[256,896]{1,0:T(8,128)(2,1)S(1)}, u32[]{:S(2)}, u32[]{:S(2)}) %collective-permute-start.26) | collective-permute-done | bytes 458784 | tf_op jit(solution)/shard_map/gather_hidden/ppermute | solution.py:17
  156.3 3.6 %collective-permute-done.24 = bf16[256,896]{1,0:T(8,128)(2,1)S(1)} collective-permute-done((bf16[256,896]{1,0:T(8,128)(2,1)S(1)}, bf16[256,896]{1,0:T(8,128)(2,1)S(1)}, u32[]{:S(2)}, u32[]{:S(2)}) %collective-permute-start.24) | collective-permute-done | bytes 458784 | tf_op jit(solution)/shard_map/gather_hidden/ppermute | solution.py:17
  159.9 9.4 %collective-permute-done.22 = bf16[256,896]{1,0:T(8,128)(2,1)S(1)} collective-permute-done((bf16[256,896]{1,0:T(8,128)(2,1)S(1)}, bf16[256,896]{1,0:T(8,128)(2,1)S(1)}, u32[]{:S(2)}, u32[]{:S(2)}) %collective-permute-start.22) | collective-permute-done | bytes 458784 | tf_op jit(solution)/shard_map/gather_hidden/ppermute | solution.py:17
  188.8 12.5 %collective-permute-done.33 = bf16[512,384]{1,0:T(8,128)(2,1)S(1)} collective-permute-done((bf16[512,384]{1,0:T(8,128)(2,1)S(1)}, bf16[512,384]{1,0:T(8,128)(2,1)S(1)}, u32[]{:S(2)}, u32[]{:S(2)}) %collective-permute-start.33) | collective-permute-done | bytes 393248 | tf_op jit(solution)/shard_map/reduce_rows/ppermute | solution.py:17
  201.2 3.7 %collective-permute-done.31 = bf16[512,384]{1,0:T(8,128)(2,1)S(1)} collective-permute-done((bf16[512,384]{1,0:T(8,128)(2,1)S(1)}, bf16[512,384]{1,0:T(8,128)(2,1)S(1)}, u32[]{:S(2)}, u32[]{:S(2)}) %collective-permute-start.31) | collective-permute-done | bytes 393248 | tf_op jit(solution)/shard_map/reduce_rows/ppermute | solution.py:17
  207.4 7.6 %collective-permute-done.36 = bf16[256,640]{1,0:T(8,128)(2,1)S(1)} collective-permute-done((bf16[256,640]{1,0:T(8,128)(2,1)S(1)}, bf16[256,640]{1,0:T(8,128)(2,1)S(1)}, u32[]{:S(2)}, u32[]{:S(2)}) %collective-permute-start.36) | collective-permute-done | bytes 327712 | tf_op jit(solution)/shard_map/reduce_rows/ppermute | solution.py:17
  219.8 5.7 %all-to-all-start.1 = ((bf16[8,64,384]{2,1,0:T(8,128)(2,1)}), bf16[8,64,384]{2,1,0:T(8,128)(2,1)S(1)}, u32[]{:S(2)}, u32[]{:S(2)}) async-start(bf16[8,64,384]{2,1,0:T(8,128)(2,1)} %bitcast.14), calls=%async_computation.2 | async-start | bytes 786432 | tf_op jit(solution)/shard_map/reduce_rows/all_to_all | solution.py:84
  230.6 7.4 %all-to-all-done.1 = bf16[8,64,384]{2,1,0:T(8,128)(2,1)S(1)} async-done(((bf16[8,64,384]{2,1,0:T(8,128)(2,1)}), bf16[8,64,384]{2,1,0:T(8,128)(2,1)S(1)}, u32[]{:S(2)}, u32[]{:S(2)}) %all-to-all-start.1) | async-done | bytes 393248 | tf_op jit(solution)/shard_map/reduce_rows/all_to_all | solution.py:84
  (193 shorter events, 79.3 us)
Async XLA Ops:
  7.2 124.1 %reduce-scatter.2.cloned.1.call-start = ((), (), s32[]{:S(2)}) async-start(), calls=%async_computation.3 | async-start | bytes 8257536 | tf_op jit(solution)/shard_map/reduce_gate_up/reduce_scatter | solution.py:150
  10.1 11.9 %collective-permute-start.2 = (bf16[64,1024]{1,0:T(8,128)(2,1)}, bf16[64,1024]{1,0:T(8,128)(2,1)S(1)}, u32[]{:S(2)}, u32[]{:S(2)}) collective-permute-start(bf16[64,1024]{1,0:T(8,128)(2,1)} %param.9), channel_id=1, source_target_pairs={{0,16},{8,24},{16,0},{24,8},{1,17},{9,25},{17,1},{25,9},{2,18},{10... | collective-permute-start | bytes 393224 | tf_op jit(solution)/shard_map/gather_tokens/ppermute | solution.py:17
  10.9 11.1 %collective-permute-start.3 = (bf16[64,1024]{1,0:T(8,128)(2,1)}, bf16[64,1024]{1,0:T(8,128)(2,1)S(1)}, u32[]{:S(2)}, u32[]{:S(2)}) collective-permute-start(bf16[64,1024]{1,0:T(8,128)(2,1)} %param.9), channel_id=1, source_target_pairs={{0,8},{8,16},{16,24},{24,0},{1,9},{9,17},{17,25},{25,1},{2,10},{10... | collective-permute-start | bytes 393224 | tf_op jit(solution)/shard_map/gather_tokens/ppermute | solution.py:17
  26.2 11.6 %collective-permute-start.8 = (bf16[128,1024]{1,0:T(8,128)(2,1)S(1)}, bf16[128,1024]{1,0:T(8,128)(2,1)S(1)}, u32[]{:S(2)}, u32[]{:S(2)}) collective-permute-start(bf16[128,1024]{1,0:T(8,128)(2,1)S(1)} %collective-permute-done.1), channel_id=1, source_target_pairs={{0,224},{32,0},{64,32},{96,64},{128,96},{160,128},{192,160},{224,1... | collective-permute-start | bytes 786440 | tf_op jit(solution)/shard_map/gather_tokens/ppermute | solution.py:17
  30.2 11.4 %collective-permute-start.12 = (bf16[128,1024]{1,0:T(8,128)(2,1)S(1)}, bf16[128,1024]{1,0:T(8,128)(2,1)S(1)}, u32[]{:S(2)}, u32[]{:S(2)}) collective-permute-start(bf16[128,1024]{1,0:T(8,128)(2,1)S(1)} %collective-permute-done.11), channel_id=1, source_target_pairs={{0,32},{32,64},{64,96},{96,128},{128,160},{160,192},{192,224},{224... | collective-permute-start | bytes 786440 | tf_op jit(solution)/shard_map/gather_tokens/ppermute | solution.py:17
  32.2 11.4 %collective-permute-start.5 = (bf16[128,1024]{1,0:T(8,128)(2,1)S(1)}, bf16[128,1024]{1,0:T(8,128)(2,1)S(1)}, u32[]{:S(2)}, u32[]{:S(2)}) collective-permute-start(bf16[128,1024]{1,0:T(8,128)(2,1)S(1)} %collective-permute-done.4), channel_id=1, source_target_pairs={{0,224},{32,0},{64,32},{96,64},{128,96},{160,128},{192,160},{224,1... | collective-permute-start | bytes 786440 | tf_op jit(solution)/shard_map/gather_tokens/ppermute | solution.py:17
  35.9 11.2 %collective-permute-start.7 = (bf16[128,1024]{1,0:T(8,128)(2,1)S(1)}, bf16[128,1024]{1,0:T(8,128)(2,1)S(1)}, u32[]{:S(2)}, u32[]{:S(2)}) collective-permute-start(bf16[128,1024]{1,0:T(8,128)(2,1)S(1)} %collective-permute-done.6), channel_id=1, source_target_pairs={{0,32},{32,64},{64,96},{96,128},{128,160},{160,192},{192,224},{224... | collective-permute-start | bytes 786440 | tf_op jit(solution)/shard_map/gather_tokens/ppermute | solution.py:17
  41.6 11.2 %collective-permute-start.14 = (bf16[128,1024]{1,0:T(8,128)(2,1)S(1)}, bf16[128,1024]{1,0:T(8,128)(2,1)S(1)}, u32[]{:S(2)}, u32[]{:S(2)}) collective-permute-start(bf16[128,1024]{1,0:T(8,128)(2,1)S(1)} %collective-permute-done.12), channel_id=1, source_target_pairs={{0,32},{32,64},{64,96},{96,128},{128,160},{160,192},{192,224},{224... | collective-permute-start | bytes 786440 | tf_op jit(solution)/shard_map/gather_tokens/ppermute | solution.py:17
  80.9 26.8 %all-to-all-start = ((bf16[32,8,1152]{2,1,0:T(8,128)(2,1)}), bf16[32,8,1152]{2,1,0:T(8,128)(2,1)S(1)}, u32[]{:S(2)}, u32[]{:S(2)}) async-start(bf16[32,8,1152]{2,1,0:T(8,128)(2,1)} %fusion.3), calls=%async_computation.1 | async-start | bytes 1179648 | tf_op jit(solution)/shard_map/exchange_gradients/all_to_all | solution.py:179
  117.5 11.1 %collective-permute-start.20 = (bf16[8,64,128]{2,1,0:T(8,128)(2,1)S(1)}, bf16[8,64,128]{2,1,0:T(8,128)(2,1)S(1)}, u32[]{:S(2)}, u32[]{:S(2)}) collective-permute-start(bf16[8,64,128]{2,1,0:T(8,128)(2,1)S(1)} %add_convert_fusion.7), channel_id=1, source_target_pairs={{0,2},{2,4},{4,6},{6,0},{1,3},{3,5},{5,7},{7,1},{8,10},{10,12},{12... | collective-permute-start | bytes 393224 | tf_op jit(solution)/shard_map/sum_low_rank/ppermute | solution.py:17
  117.5 11.1 %collective-permute-start.19 = (bf16[8,64,128]{2,1,0:T(8,128)(2,1)S(1)}, bf16[8,64,128]{2,1,0:T(8,128)(2,1)S(1)}, u32[]{:S(2)}, u32[]{:S(2)}) collective-permute-start(bf16[8,64,128]{2,1,0:T(8,128)(2,1)S(1)} %add_convert_fusion.7), channel_id=1, source_target_pairs={{0,6},{2,0},{4,2},{6,4},{1,7},{3,1},{5,3},{7,5},{8,14},{10,8},{12,... | collective-permute-start | bytes 393224 | tf_op jit(solution)/shard_map/sum_low_rank/ppermute | solution.py:17
  133.0 23.1 %collective-permute-start.26 = (bf16[256,896]{1,0:T(8,128)(2,1)S(1)}, bf16[256,896]{1,0:T(8,128)(2,1)S(1)}, u32[]{:S(2)}, u32[]{:S(2)}) collective-permute-start(bf16[256,896]{1,0:T(8,128)(2,1)S(1)} %fusion.28), channel_id=1, source_target_pairs={{0,2},{2,4},{4,6},{6,0},{1,3},{3,5},{5,7},{7,1},{8,10},{10,12},{12... | collective-permute-start | bytes 1376264 | tf_op jit(solution)/shard_map/gather_hidden/ppermute | solution.py:17
  145.0 14.9 %collective-permute-start.24 = (bf16[256,896]{1,0:T(8,128)(2,1)S(1)}, bf16[256,896]{1,0:T(8,128)(2,1)S(1)}, u32[]{:S(2)}, u32[]{:S(2)}) collective-permute-start(bf16[256,896]{1,0:T(8,128)(2,1)S(1)} %fusion.28), channel_id=1, source_target_pairs={{0,4},{2,6},{4,0},{6,2},{1,5},{3,7},{5,1},{7,3},{8,12},{10,14},{12... | collective-permute-start | bytes 1376264 | tf_op jit(solution)/shard_map/gather_hidden/ppermute | solution.py:17
  148.3 20.9 %collective-permute-start.22 = (bf16[256,896]{1,0:T(8,128)(2,1)S(1)}, bf16[256,896]{1,0:T(8,128)(2,1)S(1)}, u32[]{:S(2)}, u32[]{:S(2)}) collective-permute-start(bf16[256,896]{1,0:T(8,128)(2,1)S(1)} %fusion.28), channel_id=1, source_target_pairs={{0,6},{2,0},{4,2},{6,4},{1,7},{3,1},{5,3},{7,5},{8,14},{10,8},{12,... | collective-permute-start | bytes 1376264 | tf_op jit(solution)/shard_map/gather_hidden/ppermute | solution.py:17
  148.5 20.7 %collective-permute-start.17 = (bf16[256,896]{1,0:T(8,128)(2,1)S(1)}, bf16[256,896]{1,0:T(8,128)(2,1)S(1)}, u32[]{:S(2)}, u32[]{:S(2)}) collective-permute-start(bf16[256,896]{1,0:T(8,128)(2,1)S(1)} %fusion.28), channel_id=1, source_target_pairs={{0,1},{1,0},{2,3},{3,2},{4,5},{5,4},{6,7},{7,6},{8,9},{9,8},{10,11... | collective-permute-start | bytes 1376264 | tf_op jit(solution)/shard_map/gather_hidden/ppermute | solution.py:17
  156.1 14.8 %collective-permute-start.27 = (bf16[256,896]{1,0:T(8,128)(2,1)S(1)}, bf16[256,896]{1,0:T(8,128)(2,1)S(1)}, u32[]{:S(2)}, u32[]{:S(2)}) collective-permute-start(bf16[256,896]{1,0:T(8,128)(2,1)S(1)} %collective-permute-done.26), channel_id=1, source_target_pairs={{0,1},{1,0},{2,3},{3,2},{4,5},{5,4},{6,7},{7,6},{8,9},{9,8},{10,11... | collective-permute-start | bytes 1376264 | tf_op jit(solution)/shard_map/gather_hidden/ppermute | solution.py:17
  159.8 12.6 %collective-permute-start.25 = (bf16[256,896]{1,0:T(8,128)(2,1)S(1)}, bf16[256,896]{1,0:T(8,128)(2,1)S(1)}, u32[]{:S(2)}, u32[]{:S(2)}) collective-permute-start(bf16[256,896]{1,0:T(8,128)(2,1)S(1)} %collective-permute-done.24), channel_id=1, source_target_pairs={{0,1},{1,0},{2,3},{3,2},{4,5},{5,4},{6,7},{7,6},{8,9},{9,8},{10,11... | collective-permute-start | bytes 1376264 | tf_op jit(solution)/shard_map/gather_hidden/ppermute | solution.py:17
  176.7 11.8 %collective-permute-start.28 = (bf16[256,640]{1,0:T(8,128)(2,1)S(1)}, bf16[256,640]{1,0:T(8,128)(2,1)S(1)}, u32[]{:S(2)}, u32[]{:S(2)}) collective-permute-start(bf16[256,640]{1,0:T(8,128)(2,1)S(1)} %pad_maximum_fusion.8), channel_id=1, source_target_pairs={{0,32},{32,64},{64,96},{96,128},{128,160},{160,192},{192,224},{224... | collective-permute-start | bytes 983048 | tf_op jit(solution)/shard_map/reduce_rows/ppermute | solution.py:17
  181.0 20.2 %collective-permute-start.33 = (bf16[512,384]{1,0:T(8,128)(2,1)S(1)}, bf16[512,384]{1,0:T(8,128)(2,1)S(1)}, u32[]{:S(2)}, u32[]{:S(2)}) collective-permute-start(bf16[512,384]{1,0:T(8,128)(2,1)S(1)} %bitcast.39), channel_id=1, source_target_pairs={{0,24},{8,0},{16,8},{24,16},{1,25},{9,1},{17,9},{25,17},{2,26},{10... | collective-permute-start | bytes 1179656 | tf_op jit(solution)/shard_map/reduce_rows/ppermute | solution.py:17
  184.0 17.2 %collective-permute-start.32 = (bf16[512,384]{1,0:T(8,128)(2,1)S(1)}, bf16[512,384]{1,0:T(8,128)(2,1)S(1)}, u32[]{:S(2)}, u32[]{:S(2)}) collective-permute-start(bf16[512,384]{1,0:T(8,128)(2,1)S(1)} %bitcast.38), channel_id=1, source_target_pairs={{0,16},{8,24},{16,0},{24,8},{1,17},{9,25},{17,1},{25,9},{2,18},{10... | collective-permute-start | bytes 1179656 | tf_op jit(solution)/shard_map/reduce_rows/ppermute | solution.py:17
  184.9 20.0 %collective-permute-start.31 = (bf16[512,384]{1,0:T(8,128)(2,1)S(1)}, bf16[512,384]{1,0:T(8,128)(2,1)S(1)}, u32[]{:S(2)}, u32[]{:S(2)}) collective-permute-start(bf16[512,384]{1,0:T(8,128)(2,1)S(1)} %bitcast.37), channel_id=1, source_target_pairs={{0,8},{8,16},{16,24},{24,0},{1,9},{9,17},{17,25},{25,1},{2,10},{10... | collective-permute-start | bytes 1179656 | tf_op jit(solution)/shard_map/reduce_rows/ppermute | solution.py:17
  188.6 16.6 %collective-permute-start.29 = (bf16[256,640]{1,0:T(8,128)(2,1)S(1)}, bf16[256,640]{1,0:T(8,128)(2,1)S(1)}, u32[]{:S(2)}, u32[]{:S(2)}) collective-permute-start(bf16[256,640]{1,0:T(8,128)(2,1)S(1)} %add_convert_fusion.5), channel_id=1, source_target_pairs={{0,32},{32,64},{64,96},{96,128},{128,160},{160,192},{192,224},{224... | collective-permute-start | bytes 983048 | tf_op jit(solution)/shard_map/reduce_rows/ppermute | solution.py:17
  207.1 11.0 %collective-permute-start.34 = (bf16[256,640]{1,0:T(8,128)(2,1)S(1)}, bf16[256,640]{1,0:T(8,128)(2,1)S(1)}, u32[]{:S(2)}, u32[]{:S(2)}) collective-permute-start(bf16[256,640]{1,0:T(8,128)(2,1)S(1)} %add_convert_fusion.4), channel_id=1, source_target_pairs={{0,32},{32,64},{64,96},{96,128},{128,160},{160,192},{192,224},{224... | collective-permute-start | bytes 983048 | tf_op jit(solution)/shard_map/reduce_rows/ppermute | solution.py:17
  219.8 18.2 %all-to-all-start.1 = ((bf16[8,64,384]{2,1,0:T(8,128)(2,1)}), bf16[8,64,384]{2,1,0:T(8,128)(2,1)S(1)}, u32[]{:S(2)}, u32[]{:S(2)}) async-start(bf16[8,64,384]{2,1,0:T(8,128)(2,1)} %bitcast.14), calls=%async_computation.2 | async-start | bytes 786432 | tf_op jit(solution)/shard_map/reduce_rows/all_to_all | solution.py:84
  (32 other events, 499.0 us)
Sparse Core Ops, SparseCore 0:
  77.2 53.9 reduce-scatter.1
where the time goes:
time: 250 us; the launch traced here: 246 us
  waiting for transfers between devices  115 us (46%)
  starting transfers between devices  75.8 us (30%)
  matrix products  24.5 us (10%)
  between operations  15.3 us (6%)
  local copies, waits for them, and re-layouts  9.1 us (4%)
  other arithmetic  6.45 us (3%)
    ppermute x41, waiting for transfers between devices, from_peer(): return lax.ppermute(value, axis, [(i, (i - offset) % n) for i in range(n)])  87.6 us
    ppermute x41, starting transfers between devices, from_peer(): return lax.ppermute(value, axis, [(i, (i - offset) % n) for i in range(n)])  60.8 us
    all_to_all x1, waiting for transfers between devices, per_device(): lax.all_to_all(send, ('z', 'x'), split_axis=0, concat_axis=0, tiled=True)  17.4 us
    dot_general x1, matrix products, per_device(): jnp.dot(shard_rows, gate_up_weight, preferred_element_type=F32).astype(BF)  9.59 us
    all_to_all x1, starting transfers between devices, per_device(): lax.all_to_all(send, ('z', 'x'), split_axis=0, concat_axis=0, tiled=True)  9.19 us
    all_to_all x1, waiting for transfers between devices, exchange(): return lax.all_to_all(blocks, axis, split_axis=0, concat_axis=0, tiled=True)  7.4 us
    dot_general x4, matrix products, per_device(): jnp.dot(jnp.concatenate([piece, put[d]], 1), down_weight, preferred_eleme...  6.17 us
    all_to_all x1, starting transfers between devices, exchange(): return lax.all_to_all(blocks, axis, split_axis=0, concat_axis=0, tiled=True)  5.73 us
  transfers between devices with their start and end apart: 44, of which 25 were waited for; matrix products, arithmetic and copies ran while one was open for 9% of the time, Pallas kernels for 0%

commit v1 on v0

--- a/solution.py
+++ b/solution.py
@@ -31,7 +31,7 @@
     far = {1: n // 2, -1: (n - 1) // 2}
     moving = {sign: blocks[(sign * far[sign]) % n] for sign in far}
     for d in range(n // 2 - 1, -1, -1):
-        if d == 1:
+        if d == 0:
             moving[1], moving[-1], beside = lax.optimization_barrier((moving[1], moving[-1], beside))
         for sign in far:
             if d < far[sign]:
@@ -90,12 +90,14 @@
     near = out[:, cut:].reshape(NZ, NX, step // NX, width - cut)
     near = jnp.concatenate([near[:, d].reshape(-1, width - cut) for d in range(NX)], 0)
     near = direct_reduce(near, "x").astype(BF)
+    block = near.shape[0] // NZ
+    near = lax.dynamic_slice_in_dim(
+        jnp.concatenate([near, near], 0), (NZ - lax.axis_index("z")) % NZ * block, NZ * block, 0
+    )
     far, near = ring_reduce([out[d * step : (d + 1) * step, :cut] for d in range(NZ)], "z", near)
+    near = exchange(near.reshape(NZ, block, width - cut), "z")
+    near = jnp.sum(near.astype(F32), 0)
     far = far.astype(BF)
-    step = near.shape[0] // NZ
-    turn = (NZ - lax.axis_index("z")) % NZ * step
-    near = lax.dynamic_slice_in_dim(jnp.concatenate([near, near], 0), turn, NZ * step, 0)
-    near = jnp.sum(exchange(near.reshape(NZ, step, width - cut), "z").astype(F32), 0)
     return jnp.concatenate([direct_reduce(far, "x"), near], 1)
 
 

time: 250 us -> 250 us (level)
    all_to_all x1, waiting for transfers between devices: 7.4 us -> 3.43 us  [exchange(): return lax.all_to_all(blocks, axis, split_axis=0, concat_axis=0, tiled=True)]
  transfers between devices with their start and end apart: 44 -> 44, of which waited for: 25 -> 29; matrix products, arithmetic and copies ran while one was open for 9% -> 9% of each run, Pallas kernels for 0% -> 0%
where the time goes in v1:
time: 250 us; the launch traced here: 245 us
  waiting for transfers between devices  113 us (45%)
  starting transfers between devices  76.9 us (31%)
  matrix products  24.5 us (10%)
  between operations  15.3 us (6%)
  local copies, waits for them, and re-layouts  9.1 us (4%)
  other arithmetic  6.47 us (3%)
    ppermute x41, waiting for transfers between devices, from_peer(): return lax.ppermute(value, axis, [(i, (i - offset) % n) for i in range(n)])  89.8 us
    ppermute x41, starting transfers between devices, from_peer(): return lax.ppermute(value, axis, [(i, (i - offset) % n) for i in range(n)])  61.1 us
    all_to_all x1, waiting for transfers between devices, per_device(): lax.all_to_all(send, ('z', 'x'), split_axis=0, concat_axis=0, tiled=True)  17.4 us
    dot_general x1, matrix products, per_device(): jnp.dot(shard_rows, gate_up_weight, preferred_element_type=F32).astype(BF)  9.59 us
    all_to_all x1, starting transfers between devices, per_device(): lax.all_to_all(send, ('z', 'x'), split_axis=0, concat_axis=0, tiled=True)  9.19 us
    all_to_all x1, starting transfers between devices, exchange(): return lax.all_to_all(blocks, axis, split_axis=0, concat_axis=0, tiled=True)  6.63 us
    dot_general x4, matrix products, per_device(): jnp.dot(jnp.concatenate([piece, put[d]], 1), down_weight, preferred_eleme...  6.17 us
    unnamed x62, local copies, waits for them, and re-layouts  5.17 us
  transfers between devices with their start and end apart: 44, of which 29 were waited for; matrix products, arithmetic and copies ran while one was open for 9% of the time, Pallas kernels for 0%

profile of v1, /device:TPU:8, one launch (start us, length us, event | category | flops | bytes accessed | tf_op | source)
XLA Modules:
  0.0 245.2 jit_solution(9706209312253482135)
XLA Ops:
  16.0 5.9 %collective-permute-start.1 = (bf16[128,1024]{1,0:T(8,128)(2,1)S(1)}, bf16[128,1024]{1,0:T(8,128)(2,1)S(1)}, u32[]{:S(2)}, u32[]{:S(2)}) collective-permute-start(bf16[128,1024]{1,0:T(8,128)(2,1)S(1)} %get-tuple-element.84), channel_id=1, source_target_pairs={{0,224},{32,0},{64,32},{96,64},{128,96},{160,128},{192,160},{224,1... | collective-permute-start | bytes 786440 | tf_op jit(solution)/shard_map/gather_tokens/ppermute | solution.py:17
  22.0 3.5 %collective-permute-start.4 = (bf16[128,1024]{1,0:T(8,128)(2,1)S(1)}, bf16[128,1024]{1,0:T(8,128)(2,1)S(1)}, u32[]{:S(2)}, u32[]{:S(2)}) collective-permute-start(bf16[128,1024]{1,0:T(8,128)(2,1)S(1)} %constant_dynamic-update-slice_fusion.2), channel_id=1, source_target_pairs={{0,224},{32,0},{64,32},{96,64},{128,96},{160,128},{192,160},{224,1... | collective-permute-start | bytes 786440 | tf_op jit(solution)/shard_map/gather_tokens/ppermute | solution.py:17
  26.2 3.7 %collective-permute-start.8 = (bf16[128,1024]{1,0:T(8,128)(2,1)S(1)}, bf16[128,1024]{1,0:T(8,128)(2,1)S(1)}, u32[]{:S(2)}, u32[]{:S(2)}) collective-permute-start(bf16[128,1024]{1,0:T(8,128)(2,1)S(1)} %collective-permute-done.1), channel_id=1, source_target_pairs={{0,224},{32,0},{64,32},{96,64},{128,96},{160,128},{192,160},{224,1... | collective-permute-start | bytes 786440 | tf_op jit(solution)/shard_map/gather_tokens/ppermute | solution.py:17
  32.2 3.7 %collective-permute-start.5 = (bf16[128,1024]{1,0:T(8,128)(2,1)S(1)}, bf16[128,1024]{1,0:T(8,128)(2,1)S(1)}, u32[]{:S(2)}, u32[]{:S(2)}) collective-permute-start(bf16[128,1024]{1,0:T(8,128)(2,1)S(1)} %collective-permute-done.4), channel_id=1, source_target_pairs={{0,224},{32,0},{64,32},{96,64},{128,96},{160,128},{192,160},{224,1... | collective-permute-start | bytes 786440 | tf_op jit(solution)/shard_map/gather_tokens/ppermute | solution.py:17
  37.8 3.7 %collective-permute-done.12 = bf16[128,1024]{1,0:T(8,128)(2,1)S(1)} collective-permute-done((bf16[128,1024]{1,0:T(8,128)(2,1)S(1)}, bf16[128,1024]{1,0:T(8,128)(2,1)S(1)}, u32[]{:S(2)}, u32[]{:S(2)}) %collective-permute-start.12) | collective-permute-done | bytes 262176 | tf_op jit(solution)/shard_map/gather_tokens/ppermute | solution.py:17
  43.6 3.6 %collective-permute-done.7 = bf16[128,1024]{1,0:T(8,128)(2,1)S(1)} collective-permute-done((bf16[128,1024]{1,0:T(8,128)(2,1)S(1)}, bf16[128,1024]{1,0:T(8,128)(2,1)S(1)}, u32[]{:S(2)}, u32[]{:S(2)}) %collective-permute-start.7) | collective-permute-done | bytes 262176 | tf_op jit(solution)/shard_map/gather_tokens/ppermute | solution.py:17
  49.2 3.6 %collective-permute-done.14 = bf16[128,1024]{1,0:T(8,128)(2,1)S(1)} collective-permute-done((bf16[128,1024]{1,0:T(8,128)(2,1)S(1)}, bf16[128,1024]{1,0:T(8,128)(2,1)S(1)}, u32[]{:S(2)}, u32[]{:S(2)}) %collective-permute-start.14) | collective-permute-done | bytes 262176 | tf_op jit(solution)/shard_map/gather_tokens/ppermute | solution.py:17
  60.5 4.9 %collective-permute-done.16 = bf16[128,1024]{1,0:T(8,128)(2,1)S(1)} collective-permute-done((bf16[128,1024]{1,0:T(8,128)(2,1)S(1)}, bf16[128,1024]{1,0:T(8,128)(2,1)S(1)}, u32[]{:S(2)}, u32[]{:S(2)}) %collective-permute-start.16) | collective-permute-done | bytes 262176 | tf_op jit(solution)/shard_map/gather_tokens/ppermute | solution.py:17
  67.5 9.6 %convolution_convert_fusion = bf16[2048,1792]{1,0:T(8,128)(2,1)} fusion(bf16[2048,1024]{1,0:T(8,128)(2,1)S(1)} %constant_dynamic-update-slice_fusion.4, bf16[1024,896]{1,0:T(8,128)(2,1)S(1)} %copy-done.9, bf16[1024,896]{1,0:T(8,128)(2,1)S(1)} %copy-done.10), kind=kOutput, calls=%fused_computation | convolution fusion | flops 7527202816 | bytes 15204352 | tf_op jit(solution)/shard_map/gate_up/dot_general | solution.py:150
  80.9 9.2 %all-to-all-start = ((bf16[32,8,1152]{2,1,0:T(8,128)(2,1)}), bf16[32,8,1152]{2,1,0:T(8,128)(2,1)S(1)}, u32[]{:S(2)}, u32[]{:S(2)}) async-start(bf16[32,8,1152]{2,1,0:T(8,128)(2,1)} %fusion.3), calls=%async_computation.1 | async-start | bytes 1179648 | tf_op jit(solution)/shard_map/exchange_gradients/all_to_all | solution.py:181
  90.3 17.4 %all-to-all-done = bf16[32,8,1152]{2,1,0:T(8,128)(2,1)S(1)} async-done(((bf16[32,8,1152]{2,1,0:T(8,128)(2,1)}), bf16[32,8,1152]{2,1,0:T(8,128)(2,1)S(1)}, u32[]{:S(2)}, u32[]{:S(2)}) %all-to-all-start) | async-done | bytes 589856 | tf_op jit(solution)/shard_map/exchange_gradients/all_to_all | solution.py:181
  109.5 3.6 %fusion.5 = bf16[256,1024]{1,0:T(8,128)(2,1)S(1)} fusion(bf16[2048,1024]{1,0:T(8,128)(2,1)} %copy-done.6, s32[256]{0:T(256)S(1)} %bitcast.42), kind=kOutput, calls=%fused_computation.17 | convolution fusion | flops 1074528256 | bytes 4719616 | tf_op jit(solution)/shard_map/low_rank/dot_general | solution.py:202
  119.5 5.0 %collective-permute-done.21 = bf16[8,64,128]{2,1,0:T(8,128)(2,1)S(1)} collective-permute-done((bf16[8,64,128]{2,1,0:T(8,128)(2,1)S(1)}, bf16[8,64,128]{2,1,0:T(8,128)(2,1)S(1)}, u32[]{:S(2)}, u32[]{:S(2)}) %collective-permute-start.21) | collective-permute-done | bytes 131104 | tf_op jit(solution)/shard_map/sum_low_rank/ppermute | solution.py:17
  124.5 4.1 %collective-permute-done.20 = bf16[8,64,128]{2,1,0:T(8,128)(2,1)S(1)} collective-permute-done((bf16[8,64,128]{2,1,0:T(8,128)(2,1)S(1)}, bf16[8,64,128]{2,1,0:T(8,128)(2,1)S(1)}, u32[]{:S(2)}, u32[]{:S(2)}) %collective-permute-start.20) | collective-permute-done | bytes 131104 | tf_op jit(solution)/shard_map/sum_low_rank/ppermute | solution.py:17
  133.0 10.6 %collective-permute-start.26 = (bf16[256,896]{1,0:T(8,128)(2,1)S(1)}, bf16[256,896]{1,0:T(8,128)(2,1)S(1)}, u32[]{:S(2)}, u32[]{:S(2)}) collective-permute-start(bf16[256,896]{1,0:T(8,128)(2,1)S(1)} %fusion.28), channel_id=1, source_target_pairs={{0,2},{2,4},{4,6},{6,0},{1,3},{3,5},{5,7},{7,1},{8,10},{10,12},{12... | collective-permute-start | bytes 1376264 | tf_op jit(solution)/shard_map/gather_hidden/ppermute | solution.py:17
  145.0 3.3 %collective-permute-start.24 = (bf16[256,896]{1,0:T(8,128)(2,1)S(1)}, bf16[256,896]{1,0:T(8,128)(2,1)S(1)}, u32[]{:S(2)}, u32[]{:S(2)}) collective-permute-start(bf16[256,896]{1,0:T(8,128)(2,1)S(1)} %fusion.28), channel_id=1, source_target_pairs={{0,4},{2,6},{4,0},{6,2},{1,5},{3,7},{5,1},{7,3},{8,12},{10,14},{12... | collective-permute-start | bytes 1376264 | tf_op jit(solution)/shard_map/gather_hidden/ppermute | solution.py:17
  150.0 6.0 %collective-permute-done.26 = bf16[256,896]{1,0:T(8,128)(2,1)S(1)} collective-permute-done((bf16[256,896]{1,0:T(8,128)(2,1)S(1)}, bf16[256,896]{1,0:T(8,128)(2,1)S(1)}, u32[]{:S(2)}, u32[]{:S(2)}) %collective-permute-start.26) | collective-permute-done | bytes 458784 | tf_op jit(solution)/shard_map/gather_hidden/ppermute | solution.py:17
  156.3 3.6 %collective-permute-done.24 = bf16[256,896]{1,0:T(8,128)(2,1)S(1)} collective-permute-done((bf16[256,896]{1,0:T(8,128)(2,1)S(1)}, bf16[256,896]{1,0:T(8,128)(2,1)S(1)}, u32[]{:S(2)}, u32[]{:S(2)}) %collective-permute-start.24) | collective-permute-done | bytes 458784 | tf_op jit(solution)/shard_map/gather_hidden/ppermute | solution.py:17
  159.9 9.4 %collective-permute-done.22 = bf16[256,896]{1,0:T(8,128)(2,1)S(1)} collective-permute-done((bf16[256,896]{1,0:T(8,128)(2,1)S(1)}, bf16[256,896]{1,0:T(8,128)(2,1)S(1)}, u32[]{:S(2)}, u32[]{:S(2)}) %collective-permute-start.22) | collective-permute-done | bytes 458784 | tf_op jit(solution)/shard_map/gather_hidden/ppermute | solution.py:17
  192.1 9.2 %collective-permute-done.35 = bf16[512,384]{1,0:T(8,128)(2,1)S(1)} collective-permute-done((bf16[512,384]{1,0:T(8,128)(2,1)S(1)}, bf16[512,384]{1,0:T(8,128)(2,1)S(1)}, u32[]{:S(2)}, u32[]{:S(2)}) %collective-permute-start.35) | collective-permute-done | bytes 393248 | tf_op jit(solution)/shard_map/reduce_rows/ppermute | solution.py:17
  201.2 3.7 %collective-permute-done.33 = bf16[512,384]{1,0:T(8,128)(2,1)S(1)} collective-permute-done((bf16[512,384]{1,0:T(8,128)(2,1)S(1)}, bf16[512,384]{1,0:T(8,128)(2,1)S(1)}, u32[]{:S(2)}, u32[]{:S(2)}) %collective-permute-start.33) | collective-permute-done | bytes 393248 | tf_op jit(solution)/shard_map/reduce_rows/ppermute | solution.py:17
  207.0 9.2 %collective-permute-done.30 = bf16[256,640]{1,0:T(8,128)(2,1)S(1)} collective-permute-done((bf16[256,640]{1,0:T(8,128)(2,1)S(1)}, bf16[256,640]{1,0:T(8,128)(2,1)S(1)}, u32[]{:S(2)}, u32[]{:S(2)}) %collective-permute-start.30) | collective-permute-done | bytes 327712 | tf_op jit(solution)/shard_map/reduce_rows/ppermute | solution.py:17
  218.4 6.6 %all-to-all-start.1 = ((bf16[8,64,384]{2,1,0:T(8,128)(2,1)}), bf16[8,64,384]{2,1,0:T(8,128)(2,1)S(1)}, u32[]{:S(2)}, u32[]{:S(2)}) async-start(bf16[8,64,384]{2,1,0:T(8,128)(2,1)} %bitcast.14), calls=%async_computation.2 | async-start | bytes 786432 | tf_op jit(solution)/shard_map/reduce_rows/all_to_all | solution.py:84
  234.0 3.4 %all-to-all-done.1 = bf16[8,64,384]{2,1,0:T(8,128)(2,1)S(1)} async-done(((bf16[8,64,384]{2,1,0:T(8,128)(2,1)}), bf16[8,64,384]{2,1,0:T(8,128)(2,1)S(1)}, u32[]{:S(2)}, u32[]{:S(2)}) %all-to-all-start.1) | async-done | bytes 393248 | tf_op jit(solution)/shard_map/reduce_rows/all_to_all | solution.py:84
  (193 shorter events, 83.5 us)
Async XLA Ops:
  7.2 124.1 %reduce-scatter.2.cloned.1.call-start = ((), (), s32[]{:S(2)}) async-start(), calls=%async_computation.3 | async-start | bytes 8257536 | tf_op jit(solution)/shard_map/reduce_gate_up/reduce_scatter | solution.py:152
  10.1 11.9 %collective-permute-start.2 = (bf16[64,1024]{1,0:T(8,128)(2,1)}, bf16[64,1024]{1,0:T(8,128)(2,1)S(1)}, u32[]{:S(2)}, u32[]{:S(2)}) collective-permute-start(bf16[64,1024]{1,0:T(8,128)(2,1)} %param.9), channel_id=1, source_target_pairs={{0,16},{8,24},{16,0},{24,8},{1,17},{9,25},{17,1},{25,9},{2,18},{10... | collective-permute-start | bytes 393224 | tf_op jit(solution)/shard_map/gather_tokens/ppermute | solution.py:17
  10.9 11.1 %collective-permute-start.3 = (bf16[64,1024]{1,0:T(8,128)(2,1)}, bf16[64,1024]{1,0:T(8,128)(2,1)S(1)}, u32[]{:S(2)}, u32[]{:S(2)}) collective-permute-start(bf16[64,1024]{1,0:T(8,128)(2,1)} %param.9), channel_id=1, source_target_pairs={{0,8},{8,16},{16,24},{24,0},{1,9},{9,17},{17,25},{25,1},{2,10},{10... | collective-permute-start | bytes 393224 | tf_op jit(solution)/shard_map/gather_tokens/ppermute | solution.py:17
  26.2 11.6 %collective-permute-start.8 = (bf16[128,1024]{1,0:T(8,128)(2,1)S(1)}, bf16[128,1024]{1,0:T(8,128)(2,1)S(1)}, u32[]{:S(2)}, u32[]{:S(2)}) collective-permute-start(bf16[128,1024]{1,0:T(8,128)(2,1)S(1)} %collective-permute-done.1), channel_id=1, source_target_pairs={{0,224},{32,0},{64,32},{96,64},{128,96},{160,128},{192,160},{224,1... | collective-permute-start | bytes 786440 | tf_op jit(solution)/shard_map/gather_tokens/ppermute | solution.py:17
  30.2 11.4 %collective-permute-start.12 = (bf16[128,1024]{1,0:T(8,128)(2,1)S(1)}, bf16[128,1024]{1,0:T(8,128)(2,1)S(1)}, u32[]{:S(2)}, u32[]{:S(2)}) collective-permute-start(bf16[128,1024]{1,0:T(8,128)(2,1)S(1)} %collective-permute-done.11), channel_id=1, source_target_pairs={{0,32},{32,64},{64,96},{96,128},{128,160},{160,192},{192,224},{224... | collective-permute-start | bytes 786440 | tf_op jit(solution)/shard_map/gather_tokens/ppermute | solution.py:17
  32.2 11.4 %collective-permute-start.5 = (bf16[128,1024]{1,0:T(8,128)(2,1)S(1)}, bf16[128,1024]{1,0:T(8,128)(2,1)S(1)}, u32[]{:S(2)}, u32[]{:S(2)}) collective-permute-start(bf16[128,1024]{1,0:T(8,128)(2,1)S(1)} %collective-permute-done.4), channel_id=1, source_target_pairs={{0,224},{32,0},{64,32},{96,64},{128,96},{160,128},{192,160},{224,1... | collective-permute-start | bytes 786440 | tf_op jit(solution)/shard_map/gather_tokens/ppermute | solution.py:17
  35.9 11.2 %collective-permute-start.7 = (bf16[128,1024]{1,0:T(8,128)(2,1)S(1)}, bf16[128,1024]{1,0:T(8,128)(2,1)S(1)}, u32[]{:S(2)}, u32[]{:S(2)}) collective-permute-start(bf16[128,1024]{1,0:T(8,128)(2,1)S(1)} %collective-permute-done.6), channel_id=1, source_target_pairs={{0,32},{32,64},{64,96},{96,128},{128,160},{160,192},{192,224},{224... | collective-permute-start | bytes 786440 | tf_op jit(solution)/shard_map/gather_tokens/ppermute | solution.py:17
  41.6 11.2 %collective-permute-start.14 = (bf16[128,1024]{1,0:T(8,128)(2,1)S(1)}, bf16[128,1024]{1,0:T(8,128)(2,1)S(1)}, u32[]{:S(2)}, u32[]{:S(2)}) collective-permute-start(bf16[128,1024]{1,0:T(8,128)(2,1)S(1)} %collective-permute-done.12), channel_id=1, source_target_pairs={{0,32},{32,64},{64,96},{96,128},{128,160},{160,192},{192,224},{224... | collective-permute-start | bytes 786440 | tf_op jit(solution)/shard_map/gather_tokens/ppermute | solution.py:17
  80.9 26.8 %all-to-all-start = ((bf16[32,8,1152]{2,1,0:T(8,128)(2,1)}), bf16[32,8,1152]{2,1,0:T(8,128)(2,1)S(1)}, u32[]{:S(2)}, u32[]{:S(2)}) async-start(bf16[32,8,1152]{2,1,0:T(8,128)(2,1)} %fusion.3), calls=%async_computation.1 | async-start | bytes 1179648 | tf_op jit(solution)/shard_map/exchange_gradients/all_to_all | solution.py:181
  117.5 11.1 %collective-permute-start.20 = (bf16[8,64,128]{2,1,0:T(8,128)(2,1)S(1)}, bf16[8,64,128]{2,1,0:T(8,128)(2,1)S(1)}, u32[]{:S(2)}, u32[]{:S(2)}) collective-permute-start(bf16[8,64,128]{2,1,0:T(8,128)(2,1)S(1)} %add_convert_fusion.7), channel_id=1, source_target_pairs={{0,2},{2,4},{4,6},{6,0},{1,3},{3,5},{5,7},{7,1},{8,10},{10,12},{12... | collective-permute-start | bytes 393224 | tf_op jit(solution)/shard_map/sum_low_rank/ppermute | solution.py:17
  117.5 11.1 %collective-permute-start.19 = (bf16[8,64,128]{2,1,0:T(8,128)(2,1)S(1)}, bf16[8,64,128]{2,1,0:T(8,128)(2,1)S(1)}, u32[]{:S(2)}, u32[]{:S(2)}) collective-permute-start(bf16[8,64,128]{2,1,0:T(8,128)(2,1)S(1)} %add_convert_fusion.7), channel_id=1, source_target_pairs={{0,6},{2,0},{4,2},{6,4},{1,7},{3,1},{5,3},{7,5},{8,14},{10,8},{12,... | collective-permute-start | bytes 393224 | tf_op jit(solution)/shard_map/sum_low_rank/ppermute | solution.py:17
  133.0 23.1 %collective-permute-start.26 = (bf16[256,896]{1,0:T(8,128)(2,1)S(1)}, bf16[256,896]{1,0:T(8,128)(2,1)S(1)}, u32[]{:S(2)}, u32[]{:S(2)}) collective-permute-start(bf16[256,896]{1,0:T(8,128)(2,1)S(1)} %fusion.28), channel_id=1, source_target_pairs={{0,2},{2,4},{4,6},{6,0},{1,3},{3,5},{5,7},{7,1},{8,10},{10,12},{12... | collective-permute-start | bytes 1376264 | tf_op jit(solution)/shard_map/gather_hidden/ppermute | solution.py:17
  145.0 14.9 %collective-permute-start.24 = (bf16[256,896]{1,0:T(8,128)(2,1)S(1)}, bf16[256,896]{1,0:T(8,128)(2,1)S(1)}, u32[]{:S(2)}, u32[]{:S(2)}) collective-permute-start(bf16[256,896]{1,0:T(8,128)(2,1)S(1)} %fusion.28), channel_id=1, source_target_pairs={{0,4},{2,6},{4,0},{6,2},{1,5},{3,7},{5,1},{7,3},{8,12},{10,14},{12... | collective-permute-start | bytes 1376264 | tf_op jit(solution)/shard_map/gather_hidden/ppermute | solution.py:17
  148.3 20.9 %collective-permute-start.22 = (bf16[256,896]{1,0:T(8,128)(2,1)S(1)}, bf16[256,896]{1,0:T(8,128)(2,1)S(1)}, u32[]{:S(2)}, u32[]{:S(2)}) collective-permute-start(bf16[256,896]{1,0:T(8,128)(2,1)S(1)} %fusion.28), channel_id=1, source_target_pairs={{0,6},{2,0},{4,2},{6,4},{1,7},{3,1},{5,3},{7,5},{8,14},{10,8},{12,... | collective-permute-start | bytes 1376264 | tf_op jit(solution)/shard_map/gather_hidden/ppermute | solution.py:17
  148.5 20.7 %collective-permute-start.17 = (bf16[256,896]{1,0:T(8,128)(2,1)S(1)}, bf16[256,896]{1,0:T(8,128)(2,1)S(1)}, u32[]{:S(2)}, u32[]{:S(2)}) collective-permute-start(bf16[256,896]{1,0:T(8,128)(2,1)S(1)} %fusion.28), channel_id=1, source_target_pairs={{0,1},{1,0},{2,3},{3,2},{4,5},{5,4},{6,7},{7,6},{8,9},{9,8},{10,11... | collective-permute-start | bytes 1376264 | tf_op jit(solution)/shard_map/gather_hidden/ppermute | solution.py:17
  156.1 14.8 %collective-permute-start.27 = (bf16[256,896]{1,0:T(8,128)(2,1)S(1)}, bf16[256,896]{1,0:T(8,128)(2,1)S(1)}, u32[]{:S(2)}, u32[]{:S(2)}) collective-permute-start(bf16[256,896]{1,0:T(8,128)(2,1)S(1)} %collective-permute-done.26), channel_id=1, source_target_pairs={{0,1},{1,0},{2,3},{3,2},{4,5},{5,4},{6,7},{7,6},{8,9},{9,8},{10,11... | collective-permute-start | bytes 1376264 | tf_op jit(solution)/shard_map/gather_hidden/ppermute | solution.py:17
  159.8 12.6 %collective-permute-start.25 = (bf16[256,896]{1,0:T(8,128)(2,1)S(1)}, bf16[256,896]{1,0:T(8,128)(2,1)S(1)}, u32[]{:S(2)}, u32[]{:S(2)}) collective-permute-start(bf16[256,896]{1,0:T(8,128)(2,1)S(1)} %collective-permute-done.24), channel_id=1, source_target_pairs={{0,1},{1,0},{2,3},{3,2},{4,5},{5,4},{6,7},{7,6},{8,9},{9,8},{10,11... | collective-permute-start | bytes 1376264 | tf_op jit(solution)/shard_map/gather_hidden/ppermute | solution.py:17
  176.7 11.8 %collective-permute-start.28 = (bf16[256,640]{1,0:T(8,128)(2,1)S(1)}, bf16[256,640]{1,0:T(8,128)(2,1)S(1)}, u32[]{:S(2)}, u32[]{:S(2)}) collective-permute-start(bf16[256,640]{1,0:T(8,128)(2,1)S(1)} %pad_maximum_fusion.8), channel_id=1, source_target_pairs={{0,32},{32,64},{64,96},{96,128},{128,160},{160,192},{192,224},{224... | collective-permute-start | bytes 983048 | tf_op jit(solution)/shard_map/reduce_rows/ppermute | solution.py:17
  181.0 20.2 %collective-permute-start.35 = (bf16[512,384]{1,0:T(8,128)(2,1)S(1)}, bf16[512,384]{1,0:T(8,128)(2,1)S(1)}, u32[]{:S(2)}, u32[]{:S(2)}) collective-permute-start(bf16[512,384]{1,0:T(8,128)(2,1)S(1)} %bitcast.39), channel_id=1, source_target_pairs={{0,24},{8,0},{16,8},{24,16},{1,25},{9,1},{17,9},{25,17},{2,26},{10... | collective-permute-start | bytes 1179656 | tf_op jit(solution)/shard_map/reduce_rows/ppermute | solution.py:17
  184.0 17.2 %collective-permute-start.34 = (bf16[512,384]{1,0:T(8,128)(2,1)S(1)}, bf16[512,384]{1,0:T(8,128)(2,1)S(1)}, u32[]{:S(2)}, u32[]{:S(2)}) collective-permute-start(bf16[512,384]{1,0:T(8,128)(2,1)S(1)} %bitcast.38), channel_id=1, source_target_pairs={{0,16},{8,24},{16,0},{24,8},{1,17},{9,25},{17,1},{25,9},{2,18},{10... | collective-permute-start | bytes 1179656 | tf_op jit(solution)/shard_map/reduce_rows/ppermute | solution.py:17
  184.9 20.0 %collective-permute-start.33 = (bf16[512,384]{1,0:T(8,128)(2,1)S(1)}, bf16[512,384]{1,0:T(8,128)(2,1)S(1)}, u32[]{:S(2)}, u32[]{:S(2)}) collective-permute-start(bf16[512,384]{1,0:T(8,128)(2,1)S(1)} %bitcast.37), channel_id=1, source_target_pairs={{0,8},{8,16},{16,24},{24,0},{1,9},{9,17},{17,25},{25,1},{2,10},{10... | collective-permute-start | bytes 1179656 | tf_op jit(solution)/shard_map/reduce_rows/ppermute | solution.py:17
  188.6 16.6 %collective-permute-start.29 = (bf16[256,640]{1,0:T(8,128)(2,1)S(1)}, bf16[256,640]{1,0:T(8,128)(2,1)S(1)}, u32[]{:S(2)}, u32[]{:S(2)}) collective-permute-start(bf16[256,640]{1,0:T(8,128)(2,1)S(1)} %add_convert_fusion.5), channel_id=1, source_target_pairs={{0,32},{32,64},{64,96},{96,128},{128,160},{160,192},{192,224},{224... | collective-permute-start | bytes 983048 | tf_op jit(solution)/shard_map/reduce_rows/ppermute | solution.py:17
  188.8 18.1 %collective-permute-start.32 = (bf16[256,640]{1,0:T(8,128)(2,1)S(1)}, bf16[256,640]{1,0:T(8,128)(2,1)S(1)}, u32[]{:S(2)}, u32[]{:S(2)}) collective-permute-start(bf16[256,640]{1,0:T(8,128)(2,1)S(1)} %add_convert_fusion.2), channel_id=1, source_target_pairs={{0,224},{32,0},{64,32},{96,64},{128,96},{160,128},{192,160},{224,1... | collective-permute-start | bytes 983048 | tf_op jit(solution)/shard_map/reduce_rows/ppermute | solution.py:17
  218.4 19.0 %all-to-all-start.1 = ((bf16[8,64,384]{2,1,0:T(8,128)(2,1)}), bf16[8,64,384]{2,1,0:T(8,128)(2,1)S(1)}, u32[]{:S(2)}, u32[]{:S(2)}) async-start(bf16[8,64,384]{2,1,0:T(8,128)(2,1)} %bitcast.14), calls=%async_computation.2 | async-start | bytes 786432 | tf_op jit(solution)/shard_map/reduce_rows/all_to_all | solution.py:84
  (32 other events, 486.2 us)
Sparse Core Ops, SparseCore 0:
  77.2 53.9 reduce-scatter.1
